TPU v7x, 512 devices: a whole 4x4x16 slice. The times are simulated.
512 devices in a mesh: row: 32 (over y, x, core), col: 16 (over z).
Axes of the slice: x: 4, y: 4, z: 16, core: 2. Of those that a mesh axis runs over, the one named last changes fastest.
Arguments:
- ainv_block: float32 [4096, 4096], P('row', 'col'), as said below
- factor: float32 [2, 4096, 1024], P(None, 'row', 'col'), may hold values from -0.8 to 0.8
- block_mask: int32 [2, 32], replicated, may hold values 0 or 1
- diag_inverse: float32 [1024, 2, 1024], P('row', None, 'col'), may hold values from -6 to 6
Outputs:
- ainv_panel: float32 [1024, 2, 4096], P('col', None, 'row')
- ainv_diag: float32 [1024, 2, 1024], P('row', None, 'col')
Inputs may be any that keep to these rules, and one draw needn't show every extreme that they name: `ainv_block`: symmetric, diagonal entries between 2 and 3, off-diagonal entries of order one over the square root of 4096.
All inputs are finite; a program needn't handle non-finite values.
Results may differ from a plain program's by a relative error of at most 0.0001.
Values sent between devices are 32-bit elements; how exact they have to be, the bound alone decides.
A program may use at most 64 MiB of HBM per device.

v0:
```python
import jax
import jax.numpy as jnp
from jax import lax
from jax.sharding import PartitionSpec as P

BLOCK = 128


def from_root(block, axis, owner):
    block = jnp.where(lax.axis_index(axis) == owner, block, jnp.zeros_like(block))
    return lax.psum(block, axis)


def local(ainv_block, factor, block_mask, diag_inverse):
    col_count = lax.axis_size("col")
    row_count = lax.axis_size("row")
    ratio = row_count // col_count
    row_index = lax.axis_index("row")
    col_index = lax.axis_index("col")
    rows = factor.shape[1]
    local_blocks = rows // BLOCK
    local_mask = lax.dynamic_slice_in_dim(block_mask, row_index * local_blocks, local_blocks, 1)
    row_mask = jnp.repeat(local_mask, BLOCK, axis=1).astype(jnp.float32)
    masked = factor * row_mask[:, :, None]
    own_rows = lax.all_gather(masked, "col", axis=2, tiled=True)
    pieces = [from_root(own_rows, "row", ratio * col_index + offset) for offset in range(ratio)]
    column_rows = jnp.concatenate(pieces, axis=1)
    piece = column_rows
    summed = lax.psum_scatter(
        jnp.einsum(
            "ij,sjw->wsi",
            ainv_block,
            piece,
            precision=lax.Precision.HIGHEST,
            preferred_element_type=jnp.float32,
        ),
        "col",
        scatter_dimension=0,
        tiled=True,
    )
    ainv_panel = -(summed * row_mask[None, :, :])
    piece = own_rows
    correction = lax.psum_scatter(
        jnp.einsum(
            "siw,vsi->wsv",
            piece,
            ainv_panel,
            precision=lax.Precision.HIGHEST,
            preferred_element_type=jnp.float32,
        ),
        "row",
        scatter_dimension=0,
        tiled=True,
    )
    return (ainv_panel, diag_inverse - correction)


def solution(mesh):
    placed = (P("row", "col"), P(None, "row", "col"), P(), P("row", None, "col"))
    return jax.shard_map(
        local,
        mesh=mesh,
        in_specs=placed,
        out_specs=(P("col", None, "row"), P("row", None, "col")),
        check_vma=False,
    )
```

profile of v0, /device:TPU:1, one launch (start us, length us, event | category | flops | bytes accessed | tf_op | source)
XLA Modules:
  0.0 445.2 jit_solution(8940846543808888751)
XLA Ops:
  7.2 0.0 copy-start
  7.2 0.0 all-gather.2.cloned.1.call-start
  7.2 0.9 convert_reduce_fusion
  8.1 1.5 broadcast_multiply_fusion
  9.6 0.0 all-gather.2.cloned.1.call-update
  9.7 0.0 all-reduce.7.cloned.1.call-start
  9.7 67.8 %all-gather.2.cloned.1.call-done = f32[2,128,1024]{1,2,0:T(8,128)} async-done(((f32[2,128,64]{1,2,0:T(8,128)}), f32[2,128,1024]{1,2,0:T(8,128)}) %all-gather.2.cloned.1.call-update) | async-done | bytes 1048592 | tf_op jit(solution)/shard_map/all_gather | solution.py:25
  77.5 2.7 broadcast_select_fusion.1
  80.2 0.0 all-reduce.7.cloned.1.call-update
  80.3 0.0 reduce-scatter.2.cloned.1.call-start
  80.3 145.2 %all-reduce.7.cloned.1.call-done = (f32[2,128,1024]{1,2,0:T(8,128)}, f32[2,128,1024]{1,2,0:T(8,128)}) async-done(((f32[2,128,1024]{1,2,0:T(8,128)}, f32[2,128,1024]{1,2,0:T(8,128)}), (f32[2,128,1024]{1,2,0:T(8,128)}, f32[2,128,1024]{1,2,0:T(8,128)})) %all-reduce.7.cloned.1.call-update) | async-done | bytes 2097168 | tf_op jit(solution)/shard_map/psum | solution.py:11
  225.5 0.0 copy-done
  225.5 4.3 fusion.4
  229.8 0.0 reduce-scatter.2.cloned.1.call-update
  229.8 0.0 all-reduce.5.cloned.1.call-start
  229.9 60.2 %reduce-scatter.2.cloned.1.call-done = f32[64,2,128]{2,0,1:T(8,128)} async-done(((f32[1024,2,128]{2,0,1:T(8,128)}), f32[64,2,128]{2,0,1:T(8,128)}) %reduce-scatter.2.cloned.1.call-update) | async-done | bytes 65552 | tf_op jit(solution)/shard_map/reduce_scatter | solution.py:29
  290.1 0.9 multiply_negate_fusion
  291.0 1.2 convolution_bitcast_fusion
  292.3 1.3 copy.9
  293.6 0.0 all-reduce.5.cloned.1.call-update
  293.6 1.3 dynamic-slice
  295.5 0.7 copy.10
  296.2 141.0 %all-reduce.5.cloned.1.call-done = f32[1024,2,64]{2,1,0:T(2,128)} async-done(((f32[1024,2,64]{2,1,0:T(2,128)}), f32[1024,2,64]{2,1,0:T(2,128)}) %all-reduce.5.cloned.1.call-update) | async-done | bytes 524304
  437.2 1.4 dynamic-slice_subtract_fusion
  (4 shorter events, 0.0 us)
Async XLA Ops:
  7.2 218.3 %copy-start = (f32[128,256]{1,0:T(8,128)S(1)}, f32[128,256]{1,0:T(8,128)}, u32[]{:S(2)}) copy-start(f32[128,256]{1,0:T(8,128)} %param.4) | copy-start | bytes 393220
  7.2 70.4 %all-gather.2.cloned.1.call-start = ((), (), s32[]{:S(2)}) async-start(), calls=%async_computation.1 | async-start | bytes 1114112 | tf_op jit(solution)/shard_map/all_gather | solution.py:25
  9.7 215.8 %all-reduce.7.cloned.1.call-start = ((), (), s32[]{:S(2)}) async-start(), calls=%async_computation.4 | async-start | bytes 4194304 | tf_op jit(solution)/shard_map/psum | solution.py:11
  80.3 209.8 %reduce-scatter.2.cloned.1.call-start = ((), (), s32[]{:S(2)}) async-start(), calls=%async_computation.2 | async-start | bytes 1114112 | tf_op jit(solution)/shard_map/reduce_scatter | solution.py:29
  229.8 61.2 %copy-start.1 = (f32[2,128,1024]{1,2,0:T(8,128)S(1)}, f32[2,128,1024]{1,2,0:T(8,128)}, u32[]{:S(2)}) copy-start(f32[2,128,1024]{1,2,0:T(8,128)} %all-gather.2.cloned.1.call-done) | copy-start | bytes 3145732
  229.8 207.4 %all-reduce.5.cloned.1.call-start = ((), (), s32[]{:S(2)}) async-start(), calls=%async_computation.3 | async-start | bytes 2097152
  292.2 145.0 %copy-start.2 = (f32[32,2,64]{2,1,0:T(2,128)S(1)}, f32[32,2,64]{2,1,0:T(2,128)}, u32[]{:S(2)}) copy-start(f32[32,2,64]{2,1,0:T(2,128)} %param.7) | copy-start | bytes 49156
Sparse Core Ops, SparseCore 0:
  10.7 66.8 all-gather.1
  80.8 144.5 all-reduce.6
  230.0 60.0 reduce-scatter.1
  293.7 143.4 all-reduce.4
where the time goes:
time: 446 us; the launch traced here: 445 us
  waiting for transfers between devices  414 us (93%)
  between operations  14.5 us (3%)
  other arithmetic  7.42 us (2%)
  matrix products  5.58 us (1%)
    psum x1, waiting for transfers between devices, from_root(): return lax.psum(block, axis)  145 us
    unnamed x5, waiting for transfers between devices  141 us
    all_gather x1, waiting for transfers between devices, local(): own_rows = lax.all_gather(masked, 'col', axis=2, tiled=True)  67.8 us
    reduce_scatter x1, waiting for transfers between devices, local(): lax.psum_scatter(jnp.einsum('ij,sjw->wsi', ainv_block, piece, precision=l...  60.2 us
  transfers between devices with their start and end apart: 4, of which 4 were waited for; matrix products, arithmetic and copies ran while one was open for 0% of the time, Pallas kernels for 0%

commit v1 on v0

--- a/solution.py
+++ b/solution.py
@@ -22,7 +22,13 @@
     local_mask = lax.dynamic_slice_in_dim(block_mask, row_index * local_blocks, local_blocks, 1)
     row_mask = jnp.repeat(local_mask, BLOCK, axis=1).astype(jnp.float32)
     masked = factor * row_mask[:, :, None]
-    own_rows = lax.all_gather(masked, "col", axis=2, tiled=True)
+    moved = lax.all_to_all(
+        jnp.stack(lax.axis_size("col") * [masked], axis=0),
+        axis_name="col",
+        split_axis=0,
+        concat_axis=0,
+    )
+    own_rows = jnp.concatenate(moved, axis=2)
     pieces = [from_root(own_rows, "row", ratio * col_index + offset) for offset in range(ratio)]
     column_rows = jnp.concatenate(pieces, axis=1)
     piece = column_rows

time: 446 us -> 433 us (0.971)
  waiting for transfers between devices: 414 us -> 387 us
  starting transfers between devices: 0.16 us -> 15.9 us
    all_gather x1 -> x0, waiting for transfers between devices: 67.8 us -> none  [local(): own_rows = lax.all_gather(masked, 'col', axis=2, tiled=True)]
    all_to_all x0 -> x1, waiting for transfers between devices: none -> 44.8 us  [local(): lax.all_to_all(jnp.stack(lax.axis_size('col') * [masked], axis=0), axis_n...]
    all_to_all x0 -> x1, starting transfers between devices: none -> 15.7 us  [local(): lax.all_to_all(jnp.stack(lax.axis_size('col') * [masked], axis=0), axis_n...]
    unnamed x5 -> x4, waiting for transfers between devices: 141 us -> 141 us
where the time goes in v1:
time: 433 us
  waiting for transfers between devices  387 us (89%)
  starting transfers between devices  15.9 us (4%)
  between operations  14.5 us (3%)
  matrix products  5.58 us (1%)
  other arithmetic  5.57 us (1%)
  local copies, waits for them, and re-layouts  4.42 us (1%)
    unnamed x4, waiting for transfers between devices  141 us
    psum x1, waiting for transfers between devices, from_root(): return lax.psum(block, axis)  141 us
    reduce_scatter x1, waiting for transfers between devices, local(): lax.psum_scatter(jnp.einsum('ij,sjw->wsi', ainv_block, piece, precision=l...  60.2 us
    all_to_all x1, waiting for transfers between devices, local(): lax.all_to_all(jnp.stack(lax.axis_size('col') * [masked], axis=0), axis_n...  44.8 us
    all_to_all x1, starting transfers between devices, local(): lax.all_to_all(jnp.stack(lax.axis_size('col') * [masked], axis=0), axis_n...  15.7 us
  transfers between devices with their start and end apart: 4, of which 4 were waited for; matrix products, arithmetic and copies ran while one was open for 0% of the time, Pallas kernels for 0%

profile of v1, /device:TPU:1, one launch (start us, length us, event | category | flops | bytes accessed | tf_op | source)
XLA Modules:
  0.0 432.8 jit_solution(13041733305921323470)
XLA Ops:
  7.2 0.0 copy-start
  7.2 0.9 convert_reduce_fusion
  8.1 0.9 broadcast_multiply_fusion
  9.0 1.1 stack.2
  10.1 15.7 %all-to-all-start = ((f32[16,2,128,64]{2,3,1,0:T(8,128)}), f32[16,2,128,64]{2,3,1,0:T(8,128)S(1)}, u32[]{:S(2)}, u32[]{:S(2)}) async-start(f32[16,2,128,64]{2,3,1,0:T(8,128)} %stack.2), calls=%async_computation | async-start | bytes 2097152 | tf_op jit(solution)/shard_map/all_to_all | solution.py:25
  25.8 0.0 all-reduce.7.cloned.1.call-start
  25.9 44.8 %all-to-all-done = f32[16,2,128,64]{2,3,1,0:T(8,128)S(1)} async-done(((f32[16,2,128,64]{2,3,1,0:T(8,128)}), f32[16,2,128,64]{2,3,1,0:T(8,128)S(1)}, u32[]{:S(2)}, u32[]{:S(2)}) %all-to-all-start) | async-done | bytes 1048608 | tf_op jit(solution)/shard_map/all_to_all | solution.py:25
  70.7 0.1 copy.10
  70.8 1.4 broadcast_select_fusion.1
  72.2 0.0 all-reduce.7.cloned.1.call-update
  72.3 0.0 reduce-scatter.2.cloned.1.call-start
  72.3 140.8 %all-reduce.7.cloned.1.call-done = (f32[2,128,1024]{1,2,0:T(8,128)}, f32[2,128,1024]{1,2,0:T(8,128)}) async-done(((f32[2,128,1024]{1,2,0:T(8,128)}, f32[2,128,1024]{1,2,0:T(8,128)}), (f32[2,128,1024]{1,2,0:T(8,128)}, f32[2,128,1024]{1,2,0:T(8,128)})) %all-reduce.7.cloned.1.call-update) | async-done | bytes 2097168 | tf_op jit(solution)/shard_map/psum | solution.py:11
  213.1 4.3 %fusion.4 = f32[1024,2,128]{2,0,1:T(8,128)} fusion(f32[2,128,1024]{1,2,0:T(8,128)} %get-tuple-element.6, f32[2,128,1024]{1,2,0:T(8,128)} %get-tuple-element.7, f32[128,256]{1,0:T(8,128)S(1)} %copy-done), kind=kOutput, calls=%fused_computation.4 | convolution fusion | flops 805830656 | bytes 3276800 | tf_op jit(solution)/shard_map/ij,sjw->wsi/dot_general | solution.py:36
  217.5 0.0 reduce-scatter.2.cloned.1.call-update
  217.5 0.0 all-reduce.5.cloned.1.call-start
  217.6 60.2 %reduce-scatter.2.cloned.1.call-done = f32[64,2,128]{2,0,1:T(8,128)} async-done(((f32[1024,2,128]{2,0,1:T(8,128)}), f32[64,2,128]{2,0,1:T(8,128)}) %reduce-scatter.2.cloned.1.call-update) | async-done | bytes 65552 | tf_op jit(solution)/shard_map/reduce_scatter | solution.py:35
  277.8 0.9 multiply_negate_fusion
  278.7 1.2 convolution_bitcast_fusion
  280.0 1.3 copy.12
  281.2 0.0 all-reduce.5.cloned.1.call-update
  281.3 1.3 dynamic-slice
  283.2 0.7 copy.13
  283.9 141.0 %all-reduce.5.cloned.1.call-done = f32[1024,2,64]{2,1,0:T(2,128)} async-done(((f32[1024,2,64]{2,1,0:T(2,128)}), f32[1024,2,64]{2,1,0:T(2,128)}) %all-reduce.5.cloned.1.call-update) | async-done | bytes 524304
  424.9 1.4 dynamic-slice_subtract_fusion
  (3 shorter events, 0.0 us)
Async XLA Ops:
  7.2 206.0 %copy-start = (f32[128,256]{1,0:T(8,128)S(1)}, f32[128,256]{1,0:T(8,128)}, u32[]{:S(2)}) copy-start(f32[128,256]{1,0:T(8,128)} %param.4) | copy-start | bytes 393220
  10.1 60.6 %all-to-all-start = ((f32[16,2,128,64]{2,3,1,0:T(8,128)}), f32[16,2,128,64]{2,3,1,0:T(8,128)S(1)}, u32[]{:S(2)}, u32[]{:S(2)}) async-start(f32[16,2,128,64]{2,3,1,0:T(8,128)} %stack.2), calls=%async_computation | async-start | bytes 2097152 | tf_op jit(solution)/shard_map/all_to_all | solution.py:25
  25.8 187.3 %all-reduce.7.cloned.1.call-start = ((), (), s32[]{:S(2)}) async-start(), calls=%async_computation.4 | async-start | bytes 4194304 | tf_op jit(solution)/shard_map/psum | solution.py:11
  72.3 205.5 %reduce-scatter.2.cloned.1.call-start = ((), (), s32[]{:S(2)}) async-start(), calls=%async_computation.2 | async-start | bytes 1114112 | tf_op jit(solution)/shard_map/reduce_scatter | solution.py:35
  217.5 207.4 %all-reduce.5.cloned.1.call-start = ((), (), s32[]{:S(2)}) async-start(), calls=%async_computation.3 | async-start | bytes 2097152
  280.0 144.9 %copy-start.1 = (f32[32,2,64]{2,1,0:T(2,128)S(1)}, f32[32,2,64]{2,1,0:T(2,128)}, u32[]{:S(2)}) copy-start(f32[32,2,64]{2,1,0:T(2,128)} %param.7) | copy-start | bytes 49156
Sparse Core Ops, SparseCore 0:
  72.4 140.7 all-reduce.6
  217.6 60.1 reduce-scatter.1
  281.4 143.4 all-reduce.4
